TPU v7x, 512 devices: a whole 4x4x16 slice. The times are simulated.
512 devices in a mesh: row: 16 (over z_lo, x), col: 32 (over z_hi, y, core).
Axes of the slice: x: 4, y: 4, z: 16 (z_hi: 4, z_lo: 4; z = z_hi * 4 + z_lo), core: 2. Of those that a mesh axis runs over, the one named last changes fastest.
Arguments:
- b_diag: float32 [512, 512], P('row'), as said below
- a_diag: float32 [512, 512], P('row'), as said below
- b_panel: float32 [16384, 512], P(('row', 'col')), may hold values from -2 to 2
- a_panel: float32 [16384, 512], P(('row', 'col')), may hold values from -2 to 2
- a_trail: float32 [16384, 16384], P('row', 'col'), as said below
Outputs:
- a_diag_new: float32 [512, 512], P('row')
- l_panel: float32 [16384, 512], P(('row', 'col'))
- a_panel_new: float32 [16384, 512], P(('row', 'col'))
- a_trail_new: float32 [16384, 16384], P('row', 'col')
Inputs may be any that keep to these rules, and one draw needn't show every extreme that they name: b_diag is symmetric positive definite, its smallest eigenvalue 0.5 or more. a_diag is symmetric. a_trail is symmetric.
All inputs are finite; a program needn't handle non-finite values.
Results may differ from a plain program's by a relative error of at most 0.0001.
Values sent between devices are 32-bit elements; how exact they have to be, the bound alone decides.
A program may use at most 64 MiB of HBM per device.

v0:
```python
import jax
import jax.numpy as jnp
from jax import lax
from jax.sharding import Mesh
from jax.sharding import PartitionSpec as P

ROW = ("row_0", "row_1")
ROW_COL = ("row_0", "row_1", "col")
HIGHEST = lax.Precision.HIGHEST


def in_order(pieces, dim):
    pieces = jnp.moveaxis(pieces, 0, dim)
    lengths = pieces.shape
    return pieces.reshape(*lengths[:dim], lengths[dim] * lengths[dim + 1], *lengths[dim + 2 :])


def from_everyone(array, axis):
    copies = jnp.broadcast_to(array, (lax.axis_size(axis), *array.shape))
    return lax.all_to_all(copies, axis, split_axis=0, concat_axis=0, tiled=True)


def gathered_copies(array, axis, dim):
    return in_order(from_everyone(array, axis), dim)


def gather_in_order(array, axes, order):
    pieces = array[None]
    for k in order:
        pieces = lax.all_gather(pieces, axes[k], axis=0, tiled=True)
    block = [lax.axis_size(axes[k]) for k in reversed(order)]
    pieces = pieces.reshape(*block, *array.shape)
    turned = sorted(range(len(order)), key=lambda place: order[len(order) - 1 - place])
    return pieces.transpose(*turned, *range(len(order), pieces.ndim)).reshape(-1, *array.shape)


def gather_axes(array, axes, order, dim):
    return in_order(gather_in_order(array, axes, order), dim)


def sent_together(arrays, axis, dim, along):
    ends, at = ([], 0)
    for a in arrays[:-1]:
        at += a.shape[along]
        ends.append(at)
    both = jnp.concatenate(arrays, axis=along)
    return tuple(jnp.split(lax.all_gather(both, axis, axis=dim, tiled=True), ends, axis=along))


def spread(array, axis, root):
    mine = lax.axis_index(axis) == root
    return lax.psum(jnp.where(mine, array, jnp.zeros_like(array)), axis)


def matmul(left, right):
    return jnp.dot(left, right, precision=HIGHEST, preferred_element_type=jnp.float32)


def outer_sum(left, right):
    return lax.dot_general(
        left, right, (((1,), (1,)), ((), ())), precision=HIGHEST, preferred_element_type=jnp.float32
    )


def invert_factor(b_full):
    factor = jnp.linalg.cholesky(b_full)
    identity = jnp.eye(b_full.shape[0], dtype=b_full.dtype)
    return jax.scipy.linalg.solve_triangular(factor, identity, lower=True)


def shards(b_diag, a_diag, b_panel, a_panel, a_trail):
    piece_rows = a_diag.shape[0]
    b_full = gathered_copies(b_diag, ROW, 0)
    inverse = invert_factor(b_full)
    right_piece = matmul(a_diag, inverse.T)
    right_full = gather_axes(right_piece, ROW, (0, 1), 0)
    a_diag_full = matmul(inverse, right_full)
    grid_row = lax.axis_index(ROW)
    a_diag_new = lax.dynamic_slice_in_dim(a_diag_full, grid_row * piece_rows, piece_rows, 0)
    l_panel = matmul(b_panel, inverse.T)
    correction = 0.5 * matmul(l_panel, a_diag_full)
    mixed = matmul(a_panel, inverse.T) - correction
    a_panel_new = mixed - correction
    row_factor, row_mixed = sent_together((l_panel, mixed), "col", 0, 1)
    height = a_trail.shape[0]
    width_cols = a_trail.shape[1]
    grid_col = lax.axis_index("col")
    source_row = grid_col * width_cols // height
    start = jnp.clip(grid_col * width_cols - grid_row * height, 0, height - width_cols)
    outgoing = (
        lax.dynamic_slice_in_dim(row_factor, start, width_cols, 0),
        lax.dynamic_slice_in_dim(row_mixed, start, width_cols, 0),
    )
    col_factor, col_mixed = (
        spread(outgoing[0], ROW, source_row),
        spread(outgoing[1], ROW, source_row),
    )
    a_trail_new = a_trail - outer_sum(row_mixed, col_factor) - outer_sum(row_factor, col_mixed)
    return (a_diag_new, l_panel, a_panel_new, a_trail_new)


def solution(mesh):
    split = Mesh(mesh.devices.reshape(4, 4, mesh.shape["col"]), ("row_0", "row_1", "col"))
    return jax.shard_map(
        shards,
        mesh=split,
        in_specs=(P(ROW, None), P(ROW, None), P(ROW_COL, None), P(ROW_COL, None), P(ROW, "col")),
        out_specs=(P(ROW, None), P(ROW_COL, None), P(ROW_COL, None), P(ROW, "col")),
        check_vma=False,
    )
```

profile of v0, /device:TPU:8, one launch (start us, length us, event | category | flops | bytes accessed | tf_op | source)
XLA Modules:
  0.0 533.0 jit_solution(2031386575050240520)
XLA Ops:
  7.2 2.0 broadcast_in_dim.8
  9.1 8.5 %all-to-all-start = ((f32[16,32,512]{2,1,0:T(8,128)}), f32[16,32,512]{2,1,0:T(8,128)S(1)}, u32[]{:S(2)}, u32[]{:S(2)}) async-start(f32[16,32,512]{2,1,0:T(8,128)} %broadcast_in_dim.8), calls=%async_computation | async-start | bytes 2097152 | tf_op jit(solution)/shard_map/all_to_all | solution.py:20
  17.9 24.3 %all-to-all-done = f32[16,32,512]{2,1,0:T(8,128)S(1)} async-done(((f32[16,32,512]{2,1,0:T(8,128)}), f32[16,32,512]{2,1,0:T(8,128)S(1)}, u32[]{:S(2)}, u32[]{:S(2)}) %all-to-all-start) | async-done | bytes 1048608 | tf_op jit(solution)/shard_map/all_to_all | solution.py:20
  42.8 1.0 copy-done.2
  43.8 11.7 %cholesky.104 = f32[128,128]{1,0:T(8,128)S(1)} custom-call(f32[128,128]{1,0:T(8,128)S(1)} %cholesky.266), custom_call_target="Cholesky" | custom-call | tf_op jit(solution)/shard_map/jit(cholesky)/cholesky | solution.py:66
  55.6 9.8 %custom-call.31 = f32[1,128,128]{1,2,0:T(8,128)S(1)} custom-call(f32[1,128,128]{2,1,0:T(8,128)S(1)} %get-tuple-element.35), custom_call_target="InvertDiagBlocksLowerTriangular" | custom-call | tf_op jit(solution)/shard_map/jit(cholesky)/cholesky | solution.py:66
  65.5 1.2 constant_dynamic-update-slice_fusion.1
  66.7 1.3 convolution_subtract_fusion.3
  68.0 11.7 %cholesky.217 = f32[128,128]{1,0:T(8,128)S(1)} custom-call(f32[128,128]{1,0:T(8,128)S(1)} %cholesky.270), custom_call_target="Cholesky" | custom-call | tf_op jit(solution)/shard_map/jit(cholesky)/cholesky | solution.py:66
  79.8 10.3 %custom-call.32 = f32[1,128,128]{1,2,0:T(8,128)S(1)} custom-call(f32[1,128,128]{2,1,0:T(8,128)S(1)} %get-tuple-element.32), custom_call_target="InvertDiagBlocksLowerTriangular" | custom-call | tf_op jit(solution)/shard_map/jit(cholesky)/cholesky | solution.py:66
  90.3 1.3 convolution_subtract_fusion.4
  91.6 11.7 %cholesky.238 = f32[128,128]{1,0:T(8,128)S(1)} custom-call(f32[128,128]{1,0:T(8,128)S(1)} %cholesky.275), custom_call_target="Cholesky" | custom-call | tf_op jit(solution)/shard_map/jit(cholesky)/cholesky | solution.py:66
  103.4 0.7 compare_reduce_fusion.1
  104.0 9.8 %custom-call.33 = f32[1,128,128]{1,2,0:T(8,128)S(1)} custom-call(f32[1,128,128]{2,1,0:T(8,128)S(1)} %get-tuple-element.29), custom_call_target="InvertDiagBlocksLowerTriangular" | custom-call | tf_op jit(solution)/shard_map/jit(cholesky)/cholesky | solution.py:66
  114.0 1.2 convolution_subtract_fusion.5
  115.3 11.7 %cholesky.255 = f32[128,128]{1,0:T(8,128)S(1)} custom-call(f32[128,128]{1,0:T(8,128)S(1)} %convolution_subtract_fusion.5), custom_call_target="Cholesky" | custom-call | tf_op jit(solution)/shard_map/jit(cholesky)/cholesky | solution.py:66
  127.0 0.8 compare_reduce_fusion
  127.8 0.6 compare_reduce_fusion.2
  131.2 10.4 %while.1 = (s32[]{:T(128)}, f32[512,512]{1,0:T(8,128)S(1)}, s32[4,2]{0,1:T(2,128)S(1)}, f32[4,128,128]{2,1,0:T(8,128)}, s32[]{:T(128)}) while((s32[]{:T(128)}, f32[512,512]{1,0:T(8,128)S(1)}, s32[4,2]{0,1:T(2,128)S(1)}, f32[4,128,128]{2,1,0:T(8,128)}, s32[]{:T(128)}) %tuple.33), condition=%wide.while_cond, body=%wide.while_body.sunk | while | flops 2 | bytes 132205 | solution.py:68
  131.2 0.5 fusion.54
  131.8 2.0 bitcast_dynamic-update-slice_fusion.2
  133.8 0.5 fusion.54
  134.4 2.0 bitcast_dynamic-update-slice_fusion.2
  136.4 0.5 fusion.54
  137.0 2.0 bitcast_dynamic-update-slice_fusion.2
  139.1 0.5 fusion.54
  139.6 2.0 bitcast_dynamic-update-slice_fusion.2
  141.6 40.1 %custom-call.34 = f32[4,128,128]{1,2,0:T(8,128)S(1)} custom-call(f32[4,128,128]{2,1,0:T(8,128)} %get-tuple-element.11), custom_call_target="InvertDiagBlocksLowerTriangular" | custom-call | tf_op jit(solution)/shard_map/jit(_solve_triangular)/triangular_solve | solution.py:68
  182.9 0.4 convolution_subtract_fusion
  183.8 0.6 convolution_subtract_fusion.2
  184.4 1.3 fusion.21
  185.7 1.1 convolution_bitcast_fusion.1
  186.7 16.5 %all-gather = f32[128,512]{1,0:T(8,128)} all-gather(f32[32,512]{1,0:T(8,128)S(1)} %convolution_bitcast_fusion.1), channel_id=2, replica_groups=mesh['row_0'=4,'row_1'=4,'col'=32] {'row_0'}, dimensions={0}, use_global_device_ids=true | all-gather | bytes 327680 | tf_op jit(solution)/shard_map/all_gather | solution.py:30
  203.4 1.1 fusion.35
  204.5 30.4 %all-gather.4.cloned.1.call-done = f32[16,32,512]{2,1,0:T(8,128)} async-done(((f32[4,32,512]{2,1,0:T(8,128)}), f32[16,32,512]{2,1,0:T(8,128)}) %all-gather.4.cloned.1.call-update) | async-done | bytes 1048592 | tf_op jit(solution)/shard_map/all_gather | solution.py:30
  234.9 1.3 copy.15
  236.2 1.9 fusion.36
  238.1 0.7 convolution_multiply_fusion
  238.8 1.7 fusion.39
  240.5 0.7 pad_maximum_fusion.1
  241.5 95.3 %all-gather.6.cloned.1.call-done = f32[1024,1024]{1,0:T(8,128)} async-done(((f32[32,1024]{1,0:T(8,128)}), f32[1024,1024]{1,0:T(8,128)}) %all-gather.6.cloned.1.call-update) | async-done | bytes 4194320 | tf_op jit(solution)/shard_map/all_gather | solution.py:47
  336.8 2.7 fusion.38
  339.5 1.2 dynamic-slice_select_fusion
  340.6 1.1 dynamic-slice_select_fusion.1
  341.8 0.6 constant_dynamic-slice_fusion.1
  342.4 173.4 %all-reduce.4.cloned.1.call-done = (f32[512,512]{1,0:T(8,128)}, f32[512,512]{1,0:T(8,128)}) async-done(((f32[512,512]{1,0:T(8,128)}, f32[512,512]{1,0:T(8,128)}), (f32[512,512]{1,0:T(8,128)}, f32[512,512]{1,0:T(8,128)})) %all-reduce.4.cloned.1.call-update) | async-done | bytes 2097168 | tf_op jit(solution)/shard_map/psum | solution.py:52
  515.8 5.5 %fusion.33 = f32[1024,512]{1,0:T(8,128)S(1)} fusion(f32[512,512]{1,0:T(8,128)} %get-tuple-element.20, f32[1024,1024]{1,0:T(8,128)} %all-gather.6.cloned.1.call-done), kind=kOutput, calls=%fused_computation.78 | convolution fusion | flops 3221225472 | bytes 5242880 | tf_op jit(solution)/shard_map/dot_general | solution.py:60
  521.3 5.0 subtract_subtract_fusion
  (49 shorter events, 3.9 us)
Async XLA Ops:
  7.2 231.6 %copy-start = (f32[32,512]{1,0:T(8,128)S(1)}, f32[32,512]{1,0:T(8,128)}, u32[]{:S(2)}) copy-start(f32[32,512]{1,0:T(8,128)} %param.8) | copy-start | bytes 196612
  9.1 33.1 %all-to-all-start = ((f32[16,32,512]{2,1,0:T(8,128)}), f32[16,32,512]{2,1,0:T(8,128)S(1)}, u32[]{:S(2)}, u32[]{:S(2)}) async-start(f32[16,32,512]{2,1,0:T(8,128)} %broadcast_in_dim.8), calls=%async_computation | async-start | bytes 2097152 | tf_op jit(solution)/shard_map/all_to_all | solution.py:20
  17.6 217.3 %all-gather.4.cloned.1.call-start = ((), (), s32[]{:S(2)}) async-start(), calls=%async_computation.1 | async-start | bytes 1310720 | tf_op jit(solution)/shard_map/all_gather | solution.py:30
  42.8 1.0 copy-start.2
  181.7 1.6 copy-start.5
  182.4 3.2 copy-start.7
  183.7 19.6 %copy-start.8 = (f32[32,512]{1,0:T(8,128)S(1)}, f32[32,512]{1,0:T(8,128)}, u32[]{:S(2)}) copy-start(f32[32,512]{1,0:T(8,128)} %param.7) | copy-start | bytes 196612
  203.3 133.5 %all-gather.6.cloned.1.call-start = ((), (), s32[]{:S(2)}) async-start(), calls=%async_computation.2 | async-start | bytes 4325376 | tf_op jit(solution)/shard_map/all_gather | solution.py:47
  204.4 36.0 %copy-start.6 = (f32[512,32]{0,1:T(8,128)}, f32[512,32]{0,1:T(8,128)S(1)}, u32[]{:S(2)}) copy-start(f32[512,32]{0,1:T(8,128)S(1)} %fusion.35) | copy-start | bytes 196612
  241.2 274.6 %all-reduce.4.cloned.1.call-start = ((), (), s32[]{:S(2)}) async-start(), calls=%async_computation.3 | async-start | bytes 4194304 | tf_op jit(solution)/shard_map/psum | solution.py:52
  341.7 179.5 %copy-start.3 = (f32[1024,512]{1,0:T(8,128)S(1)}, f32[1024,512]{1,0:T(8,128)}, u32[]{:S(2)}) copy-start(f32[1024,512]{1,0:T(8,128)} %param.9) | copy-start | bytes 6291460
  515.8 5.5 %copy-start.1 = (f32[1024,1024]{1,0:T(8,128)S(1)}, f32[1024,1024]{1,0:T(8,128)}, u32[]{:S(2)}) copy-start(f32[1024,1024]{1,0:T(8,128)} %all-gather.6.cloned.1.call-done) | copy-start | bytes 12582916
  515.8 5.5 %copy-start.4 = (f32[512,512]{1,0:T(8,128)S(1)}, f32[512,512]{1,0:T(8,128)}, u32[]{:S(2)}) copy-start(f32[512,512]{1,0:T(8,128)} %get-tuple-element.21) | copy-start | bytes 3145732
Sparse Core Ops, SparseCore 0:
  203.4 31.4 all-gather.3
  241.3 95.4 all-gather.5
  341.9 173.8 all-reduce.3
where the time goes:
time: 542 us; the launch traced here: 533 us
  waiting for transfers between devices  324 us (60%)
  other arithmetic  123 us (23%)
  matrix products  26.2 us (5%)
  local copies, waits for them, and re-layouts  18.5 us (3%)
  between operations  17 us (3%)
  blocking collectives  16.5 us (3%)
  starting transfers between devices  8.8 us (2%)
    psum x1, waiting for transfers between devices, spread(): return lax.psum(jnp.where(mine, array, jnp.zeros_like(array)), axis)  173 us
    all_gather x1, waiting for transfers between devices, sent_together(): lax.all_gather(both, axis, axis=dim, tiled=True)  95.3 us
    another operation x14, other arithmetic, invert_factor(): factor = jnp.linalg.cholesky(b_full)  78.9 us
    another operation x3, other arithmetic, invert_factor(): return jax.scipy.linalg.solve_triangular(factor, identity, lower=True)  40.3 us
    all_gather x1, waiting for transfers between devices, gather_in_order(): pieces = lax.all_gather(pieces, axes[k], axis=0, tiled=True)  30.4 us
    all_to_all x1, waiting for transfers between devices, from_everyone(): return lax.all_to_all(copies, axis, split_axis=0, concat_axis=0, tiled=True)  24.3 us
    all_gather x1, blocking collectives, gather_in_order(): pieces = lax.all_gather(pieces, axes[k], axis=0, tiled=True)  16.5 us
  transfers between devices with their start and end apart: 4, of which 4 were waited for; matrix products, arithmetic and copies ran while one was open for 0% of the time, Pallas kernels for 0%

commit v1 on v0

--- a/solution.py
+++ b/solution.py
@@ -49,7 +49,7 @@
 
 def spread(array, axis, root):
     mine = lax.axis_index(axis) == root
-    return lax.psum(jnp.where(mine, array, jnp.zeros_like(array)), axis)
+    return jnp.sum(lax.all_gather(jnp.where(mine, array, jnp.zeros_like(array)), axis), axis=0)
 
 
 def matmul(left, right):

time: 542 us -> 757 us (1.40)
  the two profiles are of different devices: /device:TPU:8 before, /device:TPU:1 now
where the time goes in v1:
time: 757 us; the launch traced here: 747 us
  waiting for transfers between devices  520 us (69%)
  other arithmetic  138 us (18%)
  matrix products  28 us (4%)
  local copies, waits for them, and re-layouts  18.5 us (2%)
  between operations  17 us (2%)
  blocking collectives  15.4 us (2%)
  starting transfers between devices  9.39 us (1%)
    all_gather x2, waiting for transfers between devices, spread(): lax.all_gather(jnp.where(mine, array, jnp.zeros_like(array)), axis)  367 us
    all_gather x1, waiting for transfers between devices, sent_together(): lax.all_gather(both, axis, axis=dim, tiled=True)  97.9 us
    another operation x14, other arithmetic, invert_factor(): factor = jnp.linalg.cholesky(b_full)  79 us
    another operation x3, other arithmetic, invert_factor(): return jax.scipy.linalg.solve_triangular(factor, identity, lower=True)  40.3 us
    all_gather x1, waiting for transfers between devices, gather_in_order(): pieces = lax.all_gather(pieces, axes[k], axis=0, tiled=True)  33.5 us
    all_to_all x1, waiting for transfers between devices, from_everyone(): return lax.all_to_all(copies, axis, split_axis=0, concat_axis=0, tiled=True)  21.8 us
    reduce_sum x2, other arithmetic, spread(): jnp.sum(lax.all_gather(jnp.where(mine, array, jnp.zeros_like(array)), axi...  15.8 us
    all_gather x1, blocking collectives, gather_in_order(): pieces = lax.all_gather(pieces, axes[k], axis=0, tiled=True)  15.4 us
  transfers between devices with their start and end apart: 5, of which 5 were waited for; matrix products, arithmetic and copies ran while one was open for 1% of the time, Pallas kernels for 0%

profile of v1, /device:TPU:1, one launch (start us, length us, event | category | flops | bytes accessed | tf_op | source)
XLA Modules:
  0.0 747.0 jit_solution(9643035117887013604)
XLA Ops:
  7.2 2.0 broadcast_in_dim.8
  9.1 9.0 %all-to-all-start = ((f32[16,32,512]{2,1,0:T(8,128)}), f32[16,32,512]{2,1,0:T(8,128)S(1)}, u32[]{:S(2)}, u32[]{:S(2)}) async-start(f32[16,32,512]{2,1,0:T(8,128)} %broadcast_in_dim.8), calls=%async_computation | async-start | bytes 2097152 | tf_op jit(solution)/shard_map/all_to_all | solution.py:20
  18.4 21.8 %all-to-all-done = f32[16,32,512]{2,1,0:T(8,128)S(1)} async-done(((f32[16,32,512]{2,1,0:T(8,128)}), f32[16,32,512]{2,1,0:T(8,128)S(1)}, u32[]{:S(2)}, u32[]{:S(2)}) %all-to-all-start) | async-done | bytes 1048608 | tf_op jit(solution)/shard_map/all_to_all | solution.py:20
  40.9 1.0 copy-done.3
  41.8 11.7 %cholesky.104 = f32[128,128]{1,0:T(8,128)S(1)} custom-call(f32[128,128]{1,0:T(8,128)S(1)} %cholesky.266), custom_call_target="Cholesky" | custom-call | tf_op jit(solution)/shard_map/jit(cholesky)/cholesky | solution.py:66
  53.6 9.8 %custom-call.31 = f32[1,128,128]{1,2,0:T(8,128)S(1)} custom-call(f32[1,128,128]{2,1,0:T(8,128)S(1)} %get-tuple-element.33), custom_call_target="InvertDiagBlocksLowerTriangular" | custom-call | tf_op jit(solution)/shard_map/jit(cholesky)/cholesky | solution.py:66
  63.5 1.2 constant_dynamic-update-slice_fusion.1
  64.8 1.3 convolution_subtract_fusion.3
  66.1 11.7 %cholesky.217 = f32[128,128]{1,0:T(8,128)S(1)} custom-call(f32[128,128]{1,0:T(8,128)S(1)} %cholesky.270), custom_call_target="Cholesky" | custom-call | tf_op jit(solution)/shard_map/jit(cholesky)/cholesky | solution.py:66
  77.8 10.3 %custom-call.32 = f32[1,128,128]{1,2,0:T(8,128)S(1)} custom-call(f32[1,128,128]{2,1,0:T(8,128)S(1)} %get-tuple-element.30), custom_call_target="InvertDiagBlocksLowerTriangular" | custom-call | tf_op jit(solution)/shard_map/jit(cholesky)/cholesky | solution.py:66
  88.3 1.3 convolution_subtract_fusion.4
  89.6 11.7 %cholesky.238 = f32[128,128]{1,0:T(8,128)S(1)} custom-call(f32[128,128]{1,0:T(8,128)S(1)} %cholesky.275), custom_call_target="Cholesky" | custom-call | tf_op jit(solution)/shard_map/jit(cholesky)/cholesky | solution.py:66
  101.4 0.7 compare_reduce_fusion.1
  102.1 9.8 %custom-call.33 = f32[1,128,128]{1,2,0:T(8,128)S(1)} custom-call(f32[1,128,128]{2,1,0:T(8,128)S(1)} %get-tuple-element.27), custom_call_target="InvertDiagBlocksLowerTriangular" | custom-call | tf_op jit(solution)/shard_map/jit(cholesky)/cholesky | solution.py:66
  112.1 1.2 convolution_subtract_fusion.5
  113.4 11.7 %cholesky.255 = f32[128,128]{1,0:T(8,128)S(1)} custom-call(f32[128,128]{1,0:T(8,128)S(1)} %convolution_subtract_fusion.5), custom_call_target="Cholesky" | custom-call | tf_op jit(solution)/shard_map/jit(cholesky)/cholesky | solution.py:66
  125.1 0.8 compare_reduce_fusion
  125.9 0.6 compare_reduce_fusion.2
  129.3 10.4 %while.1 = (s32[]{:T(128)}, f32[512,512]{1,0:T(8,128)S(1)}, s32[4,2]{0,1:T(2,128)S(1)}, f32[4,128,128]{2,1,0:T(8,128)}, s32[]{:T(128)}) while((s32[]{:T(128)}, f32[512,512]{1,0:T(8,128)S(1)}, s32[4,2]{0,1:T(2,128)S(1)}, f32[4,128,128]{2,1,0:T(8,128)}, s32[]{:T(128)}) %tuple.33), condition=%wide.while_cond, body=%wide.while_body.sunk | while | flops 2 | bytes 132205 | solution.py:68
  129.4 0.5 fusion.54
  129.9 2.0 bitcast_dynamic-update-slice_fusion.2
  132.5 2.0 bitcast_dynamic-update-slice_fusion.2
  135.1 2.0 bitcast_dynamic-update-slice_fusion.2
  137.7 2.0 bitcast_dynamic-update-slice_fusion.2
  139.8 40.1 %custom-call.34 = f32[4,128,128]{1,2,0:T(8,128)S(1)} custom-call(f32[4,128,128]{2,1,0:T(8,128)} %get-tuple-element.11), custom_call_target="InvertDiagBlocksLowerTriangular" | custom-call | tf_op jit(solution)/shard_map/jit(_solve_triangular)/triangular_solve | solution.py:68
  181.5 1.3 fusion.22
  182.8 0.6 convolution_subtract_fusion.2
  183.4 1.3 fusion.21
  184.7 1.1 convolution_bitcast_fusion.1
  185.8 15.4 %all-gather = f32[128,512]{1,0:T(8,128)} all-gather(f32[32,512]{1,0:T(8,128)S(1)} %convolution_bitcast_fusion.1), channel_id=2, replica_groups=mesh['row_0'=4,'row_1'=4,'col'=32] {'row_0'}, dimensions={0}, use_global_device_ids=true | all-gather | bytes 327680 | tf_op jit(solution)/shard_map/all_gather | solution.py:30
  201.3 1.1 fusion.35
  202.3 33.5 %all-gather.8.cloned.1.call-done = f32[16,32,512]{2,1,0:T(8,128)} async-done(((f32[4,32,512]{2,1,0:T(8,128)}), f32[16,32,512]{2,1,0:T(8,128)}) %all-gather.8.cloned.1.call-update) | async-done | bytes 1048592 | tf_op jit(solution)/shard_map/all_gather | solution.py:30
  235.9 1.3 copy.15
  237.2 1.9 fusion.36
  239.0 0.7 convolution_multiply_fusion
  239.8 1.7 fusion.39
  241.5 0.7 pad_maximum_fusion.1
  242.2 97.9 %all-gather.10.cloned.1.call-done = f32[1024,1024]{1,0:T(8,128)} async-done(((f32[32,1024]{1,0:T(8,128)}), f32[1024,1024]{1,0:T(8,128)}) %all-gather.10.cloned.1.call-update) | async-done | bytes 4194320 | tf_op jit(solution)/shard_map/all_gather | solution.py:47
  340.2 2.7 fusion.38
  342.8 1.1 dynamic-slice_select_fusion.1
  344.3 1.1 dynamic-slice_select_fusion
  345.4 0.6 constant_dynamic-slice_fusion.1
  346.1 184.2 %all-gather.12.cloned.1.call-done = f32[8192,512]{1,0:T(8,128)} async-done(((f32[512,512]{1,0:T(8,128)}), f32[8192,512]{1,0:T(8,128)}) %all-gather.12.cloned.1.call-update) | async-done | bytes 16777232 | tf_op jit(solution)/shard_map/all_gather | solution.py:52
  530.2 7.9 %reduce_sum.18 = f32[512,512]{1,0:T(8,128)S(1)} reduce(f32[16,512,512]{2,1,0:T(8,128)} %bitcast.72, f32[]{:T(128)} %constant.167.clone.1), dimensions={0}, to_apply=%region_8.9 | reduce | flops 3932160 | bytes 17825796 | tf_op jit(solution)/shard_map/reduce_sum | solution.py:52
  538.1 182.7 %all-gather.14.cloned.1.call-done = f32[8192,512]{1,0:T(8,128)} async-done(((f32[512,512]{1,0:T(8,128)}), f32[8192,512]{1,0:T(8,128)}) %all-gather.14.cloned.1.call-update) | async-done | bytes 16777232 | tf_op jit(solution)/shard_map/all_gather | solution.py:52
  720.8 7.9 %reduce_sum.19 = f32[512,512]{1,0:T(8,128)S(1)} reduce(f32[16,512,512]{2,1,0:T(8,128)} %bitcast.73, f32[]{:T(128)} %constant.167.clone.1), dimensions={0}, to_apply=%region_9.10 | reduce | flops 3932160 | bytes 17825796 | tf_op jit(solution)/shard_map/reduce_sum | solution.py:52
  728.8 5.2 fusion.33
  734.0 6.2 subtract_subtract_fusion
  (52 shorter events, 5.5 us)
Async XLA Ops:
  7.2 232.6 %copy-start = (f32[32,512]{1,0:T(8,128)S(1)}, f32[32,512]{1,0:T(8,128)}, u32[]{:S(2)}) copy-start(f32[32,512]{1,0:T(8,128)} %param.8) | copy-start | bytes 196612
  9.1 31.1 %all-to-all-start = ((f32[16,32,512]{2,1,0:T(8,128)}), f32[16,32,512]{2,1,0:T(8,128)S(1)}, u32[]{:S(2)}, u32[]{:S(2)}) async-start(f32[16,32,512]{2,1,0:T(8,128)} %broadcast_in_dim.8), calls=%async_computation | async-start | bytes 2097152 | tf_op jit(solution)/shard_map/all_to_all | solution.py:20
  18.2 217.7 %all-gather.8.cloned.1.call-start = ((), (), s32[]{:S(2)}) async-start(), calls=%async_computation.1 | async-start | bytes 1310720 | tf_op jit(solution)/shard_map/all_gather | solution.py:30
  40.9 1.0 copy-start.3
  179.9 0.7 copy-start.4
  180.6 4.1 copy-start.6
  182.7 18.5 %copy-start.7 = (f32[32,512]{1,0:T(8,128)S(1)}, f32[32,512]{1,0:T(8,128)}, u32[]{:S(2)}) copy-start(f32[32,512]{1,0:T(8,128)} %param.7) | copy-start | bytes 196612
  201.2 139.0 %all-gather.10.cloned.1.call-start = ((), (), s32[]{:S(2)}) async-start(), calls=%async_computation.2 | async-start | bytes 4325376 | tf_op jit(solution)/shard_map/all_gather | solution.py:47
  202.3 39.1 %copy-start.5 = (f32[512,32]{0,1:T(8,128)}, f32[512,32]{0,1:T(8,128)S(1)}, u32[]{:S(2)}) copy-start(f32[512,32]{0,1:T(8,128)S(1)} %fusion.35) | copy-start | bytes 196612
  242.2 288.1 %all-gather.12.cloned.1.call-start = ((), (), s32[]{:S(2)}) async-start(), calls=%async_computation.3 | async-start | bytes 17825792 | tf_op jit(solution)/shard_map/all_gather | solution.py:52
  344.0 376.9 %all-gather.14.cloned.1.call-start = ((), (), s32[]{:S(2)}) async-start(), calls=%async_computation.4 | async-start | bytes 17825792 | tf_op jit(solution)/shard_map/all_gather | solution.py:52
  728.8 5.2 copy-start.2
  734.0 6.2 copy-start.1
Sparse Core Ops, SparseCore 0:
  201.3 34.5 all-gather.7
  242.3 97.8 all-gather.9
  344.1 186.0 all-gather.11
  532.2 188.6 all-gather.13
